TPU v7x, 32 devices: a whole 2x2x4 slice. The times are simulated.
32 devices in a mesh: space: 16 (over z, y, x), sub: 2 (over core).
Axes of the slice: x: 2, y: 2, z: 4, core: 2. Of those that a mesh axis runs over, the one named last changes fastest.
Arguments:
- fluid_state: float32 [8, 65536], P(None, 'space'), may hold values from 0 to 1
- sphere_state: float32 [7, 65536], P(None, 'space'), may hold values from 0 to 1
- sphere_offset: float32 [3, 65536], P(None, 'space'), may hold values from -1 to 1
- tile_list: int32 [4096, 2], P(('space', 'sub')), may hold values from 0 to 31, as said below
- tile_count: int32 [32], P(('space', 'sub')), may hold values from 32 to 128, as said below
- clump_ids: int32 [65536], P('space'), may hold values from 0 to 127, as said below
- clump_state: float32 [6, 2048], P(None, 'space'), may hold values from -6 to 6
- clump_inverse: float32 [4, 2048], P(None, 'space'), may hold values from 0.02 to 0.2
Outputs:
- clump_velocity: float32 [6, 2048], P(None, 'space')
- sphere_velocity: float32 [3, 65536], P(None, 'space')
Inputs may be any that keep to these rules, and one draw needn't show every extreme that they name: `tile_list`: within a domain the 256 slots of its two devices name distinct pairs; the first entry is below 32, the second below 32. `tile_count`: some device's list is full in every draw. `clump_ids`: among the spheres sent to one owner from all domains, each clump id names exactly 32 spheres.
All inputs are finite; a program needn't handle non-finite values.
Results may differ from a plain program's by a relative error of at most 0.0003.
Values sent between devices are 32-bit elements; how exact they have to be, the bound alone decides.
No kernel may reach another device: no remote copies, remote signals or barrier semaphores. Data moves between devices by JAX's collectives and lax.ppermute only.
A program may use at most 64 MiB of HBM per device.

v0:
```python
import functools
import math

import jax
import jax.numpy as jnp
from jax import lax
from jax.experimental import pallas as pl
from jax.experimental.pallas import tpu as pltpu
from jax.sharding import PartitionSpec as P

TILE = 128
SLOT = 256
UNROLL = 8

support_radius = 0.5
press_coef = 4.0
visc_coef = 1.0
gravity_step = 0.1

f32 = jnp.float32
bf16 = jnp.bfloat16


def split_two(value):
    high = value.astype(bf16)
    return high, (value - high.astype(f32)).astype(bf16)


def cross(left, right):
    return [
        left[1] * right[2] - left[2] * right[1],
        left[2] * right[0] - left[0] * right[2],
        left[0] * right[1] - left[1] * right[0],
    ]


def put_rows(ref, owner, rows, clumps):
    for half in range(2):
        for k in range(3):
            ref[2 * owner + half, :, k * clumps : (k + 1) * clumps] = rows[3 * half + k : 3 * half + k + 1]


def get_rows(ref, owner, clumps):
    return [
        ref[2 * owner + half, :, k * clumps : (k + 1) * clumps] for half in range(2) for k in range(3)
    ]


def group_of(owners):
    return math.gcd(owners, 16)


def loads_kernel(
    count_ref, list_hbm, fluid_hbm, sphere_hbm, offset_hbm, ids_hbm, out_ref,
    list_ref, fluid_ref, sphere_ref, offset_ref, ids_ref, arrived,
    place_ref, wide_ref, terms_ref, weight_ref, acc_ref,
):
    fluid_tiles = fluid_ref.shape[1] // TILE
    clumps = out_ref.shape[2] // 3
    owners = out_ref.shape[0] // 2

    pairs = (
        (fluid_hbm, fluid_ref),
        (sphere_hbm, sphere_ref),
        (list_hbm, list_ref),
        (offset_hbm, offset_ref),
        (ids_hbm, ids_ref),
    )
    copies = [
        pltpu.make_async_copy(source, target, arrived.at[k]) for k, (source, target) in enumerate(pairs)
    ]
    for copy in copies:
        copy.start()

    acc_ref[...] = jnp.zeros_like(acc_ref)
    copies[0].wait()

    @pl.loop(0, fluid_tiles, unroll=8)
    def _(tile):
        cols = pl.ds(pl.multiple_of(tile * TILE, TILE), TILE)
        state = fluid_ref[:, cols]
        row = lax.broadcasted_iota(jnp.int32, state.shape, 0)
        state = jnp.where(row < 3, state * (1.0 / support_radius) - 1.0, state)
        mass = state[7:8]
        first = jnp.where(row < 7, state * mass, state)
        second = jnp.where(row < 3, state * (mass * state[6:7]), 0.0)
        high, low = split_two(jnp.concatenate([first, second], axis=0))
        both = jnp.concatenate([high, low], axis=0)
        terms_ref[tile] = jnp.concatenate([both, both], axis=1)
        turned = state.T
        for k in range(3):
            wide_ref[k, cols, :] = jnp.broadcast_to(turned[:, k : k + 1], (TILE, TILE))

    copies[1].wait()
    place_ref[...] = sphere_ref[0:3, :] * (1.0 / support_radius) - 1.0
    copies[2].wait()

    def pair_weights(slot, part):
        a = list_ref[0, slot]
        b = list_ref[1, slot]
        cols = pl.ds(pl.multiple_of(a * TILE, TILE), TILE)
        rows = pl.ds(pl.multiple_of(b * TILE, TILE), TILE)
        dx = place_ref[0:1, cols] - wide_ref[0, rows, :]
        dy = place_ref[1:2, cols] - wide_ref[1, rows, :]
        dz = place_ref[2:3, cols] - wide_ref[2, rows, :]
        square = jnp.maximum(dx * dx + dy * dy + dz * dz, 1e-30)
        falloff = jnp.maximum(1.0 - square * lax.rsqrt(square), 0.0)
        high, low = split_two(falloff * falloff * falloff)
        weight_ref[part, 0:TILE, :] = high
        weight_ref[part, TILE:, :] = low

    def add_sums(slot, part, live):
        a = list_ref[0, slot]
        b = list_ref[1, slot]
        cols = pl.ds(pl.multiple_of(a * TILE, TILE), TILE)
        sums = jnp.dot(terms_ref[b], weight_ref[part], preferred_element_type=f32)
        acc_ref[:, cols] += live * (sums[0:16] + sums[16:32])

    count = count_ref[0]
    trips = (count + UNROLL - 1) // UNROLL
    last = list_ref.shape[1] - 1

    for part in range(UNROLL):
        pair_weights(min(part, last), part)

    @pl.loop(1, trips)
    def _(trip):
        for part in range(UNROLL):
            add_sums((trip - 1) * UNROLL + part, part, 1.0)
        for part in range(UNROLL):
            pair_weights(jnp.minimum(trip * UNROLL + part, last), part)

    for part in range(UNROLL):
        slot = (trips - 1) * UNROLL + part
        live = jnp.where(slot < count, 1.0, 0.0).astype(f32)
        add_sums(jnp.clip(slot, 0, last), part, live)

    copies[3].wait()
    copies[4].wait()
    group = group_of(owners)
    width = group * SLOT

    @pl.loop(0, owners // group)
    def _(block):
        cols = pl.ds(pl.multiple_of(block * width, width), width)
        acc = acc_ref[:, cols]
        place = place_ref[:, cols]
        sphere = sphere_ref[:, cols]
        offset = offset_ref[:, cols]
        total = acc[7:8]
        pull = total * place - acc[0:3]
        press = acc[6:7] * place - acc[8:11]
        scale = press_coef * support_radius
        force = scale * (sphere[6:7] * pull + press) + visc_coef * (acc[3:6] - total * sphere[3:6])
        force = [force[k : k + 1] for k in range(3)]
        turn = cross([offset[k : k + 1] for k in range(3)], force)
        loads = jnp.concatenate(force + turn + [jnp.zeros_like(force[0])] * 2, axis=0)
        high, low = split_two(loads)
        both = jnp.concatenate([high, low], axis=0)
        column = lax.broadcasted_iota(jnp.int32, (clumps, SLOT), 0)
        for k in range(group):
            here = pl.ds(pl.multiple_of(block * width + k * SLOT, SLOT), SLOT)
            one_hot = jnp.where(column == ids_ref[:, here], 1.0, 0.0).astype(bf16)
            sums = lax.dot_general(
                both[:, k * SLOT : (k + 1) * SLOT], one_hot, (((1,), (1,)), ((), ())),
                preferred_element_type=f32,
            )
            put_rows(out_ref, block * group + k, sums[0:8] + sums[8:16], clumps)


def update_kernel(arrived_ref, state_ref, inverse_ref, out_ref):
    devices, _, width = out_ref.shape
    clumps = width // 3
    totals = jnp.sum(arrived_ref[...], axis=0)
    first = lax.axis_index("sub") == 0
    for k in range(3):
        cols = slice(k * clumps, (k + 1) * clumps)
        state = jnp.where(first, state_ref[k : k + 1, :], state_ref[k + 3 : k + 4, :])
        factor = jnp.where(first, inverse_ref[0:1, :], inverse_ref[k + 1 : k + 2, :])
        row = state + factor * totals[:, cols]
        if k == 2:
            row = row + jnp.where(first, -gravity_step, 0.0)
        out_ref[:, :, cols] = jnp.broadcast_to(row[None], (devices, 1, clumps))


def velocity_kernel(velocity_ref, offset_ref, ids_ref, clump_ref, sphere_ref):
    owners = velocity_ref.shape[0] // 2
    clumps = velocity_ref.shape[2] // 3
    group = group_of(owners)
    me = lax.axis_index("space")

    @pl.loop(0, owners // group)
    def _(block):
        for k in range(group):
            owner = block * group + k
            rows = get_rows(velocity_ref, owner, clumps) + [jnp.zeros((2, clumps), f32)]
            both = jnp.concatenate(split_two(jnp.concatenate(rows, axis=0)), axis=0)
            here = pl.ds(pl.multiple_of(owner * SLOT, SLOT), SLOT)
            column = lax.broadcasted_iota(jnp.int32, (clumps, SLOT), 0)
            one_hot = jnp.where(column == ids_ref[:, here], 1.0, 0.0).astype(bf16)
            picked = jnp.dot(both, one_hot, preferred_element_type=f32)
            picked = picked[0:8] + picked[8:16]
            offset = offset_ref[:, here]
            turn = cross([picked[3 + i : 4 + i] for i in range(3)], [offset[i : i + 1] for i in range(3)])
            sphere_ref[:, here] = picked[0:3] + jnp.concatenate(turn, axis=0)

    clump_ref[...] = jnp.concatenate(get_rows(velocity_ref, me, clumps), axis=0)


def per_device(
    fluid_state, sphere_state, sphere_offset, tile_list, tile_count, clump_ids, clump_state, clump_inverse
):
    owners = lax.axis_size("space")
    devices = owners * lax.axis_size("sub")
    spheres = sphere_state.shape[1]
    fluid = fluid_state.shape[1]
    clumps = clump_state.shape[1]
    slots = tile_list.shape[0]
    ids = clump_ids.reshape(1, spheres)
    vmem = pl.BlockSpec(memory_space=pltpu.VMEM)
    hbm = pl.BlockSpec(memory_space=pltpu.HBM)
    params = pltpu.CompilerParams(vmem_limit_bytes=48 * 1024 * 1024)

    partial = pl.pallas_call(
        loads_kernel,
        out_shape=pltpu.VMEM((devices, 1, 3 * clumps), f32),
        in_specs=[pl.BlockSpec(memory_space=pltpu.SMEM)] + [hbm] * 5,
        out_specs=vmem,
        scratch_shapes=[
            pltpu.SMEM((2, slots), jnp.int32),
            pltpu.VMEM((8, fluid), f32),
            pltpu.VMEM((7, spheres), f32),
            pltpu.VMEM((3, spheres), f32),
            pltpu.VMEM((1, spheres), jnp.int32),
            pltpu.SemaphoreType.DMA((5,)),
            pltpu.VMEM((3, spheres), f32),
            pltpu.VMEM((3, fluid, TILE), f32),
            pltpu.VMEM((fluid // TILE, 32, 2 * TILE), bf16),
            pltpu.VMEM((UNROLL, 2 * TILE, TILE), bf16),
            pltpu.VMEM((16, spheres), f32),
        ],
        compiler_params=params,
        name="clump_loads",
    )(tile_count, *(
        pltpu.with_memory_space_constraint(value, pltpu.HBM)
        for value in (tile_list.T, fluid_state, sphere_state, sphere_offset, ids)
    ))

    axes = ("space", "sub")
    arrived = lax.all_to_all(partial, axes, split_axis=0, concat_axis=0, tiled=True)
    rows = pl.pallas_call(
        update_kernel,
        out_shape=jax.ShapeDtypeStruct((devices, 1, 3 * clumps), f32),
        in_specs=[vmem] * 3,
        out_specs=vmem,
        compiler_params=params,
        name="clump_update",
    )(arrived, clump_state, clump_inverse)
    velocities = lax.all_to_all(rows, axes, split_axis=0, concat_axis=0, tiled=True)

    return pl.pallas_call(
        velocity_kernel,
        out_shape=(
            jax.ShapeDtypeStruct((6, clumps), f32),
            jax.ShapeDtypeStruct((3, spheres), f32),
        ),
        in_specs=[vmem] * 3,
        out_specs=(vmem, vmem),
        compiler_params=params,
        name="sphere_velocities",
    )(velocities, sphere_offset, ids)


def solution(mesh):
    in_specs = (
        P(None, "space"),
        P(None, "space"),
        P(None, "space"),
        P(("space", "sub"), None),
        P(("space", "sub")),
        P("space"),
        P(None, "space"),
        P(None, "space"),
    )
    out_specs = (P(None, "space"), P(None, "space"))
    return jax.shard_map(
        per_device, mesh=mesh, in_specs=in_specs, out_specs=out_specs, check_vma=False
    )
```

profile of v0, /device:TPU:0, one launch (start us, length us, event | category | flops | bytes accessed | tf_op | source)
XLA Modules:
  0.0 33.4 jit_solution(8140909851528158386)
XLA Ops:
  1.3 6.4 %clump_loads.1 = f32[32,1,384]{2,1,0:T(1,128)S(1)} custom-call(s32[1]{0:T(128)S(6)} %copy.10.count_ref, s32[2,128]{1,0:T(2,128)} %bitcast.4, f32[8,4096]{1,0:T(8,128)} %fluid_hbm.1, f32[7,4096]{1,0:T(8,128)} %sphere_hbm.1, f32[3,4096]{1,0:T(4,128)} %offset_ref.1, s32[1,4096]{1,0:T(1,128)} %bitcast.2), custom_call_target="tpu_custom_call" | custom-call | tf_op jit(solution)/shard_map/clump_loads/pallas_call | solution.py:224
  7.7 0.0 copy-start.2
  7.7 0.0 copy-start.3
  7.7 15.6 %all_to_all.10.arrived_ref = f32[32,1,384]{2,1,0:T(1,128)S(1)} all-to-all(f32[32,1,384]{2,1,0:T(1,128)S(1)} %clump_loads.1), channel_id=1, replica_groups=mesh['space'=16,'sub'=2] {'space','sub'}, dimensions={0} | all-to-all | bytes 98304 | tf_op jit(solution)/shard_map/all_to_all | solution.py:250
  23.3 0.0 copy-done.2
  23.3 0.0 copy-done.3
  23.3 0.1 clump_update.1
  23.3 0.0 copy-start
  23.3 0.0 copy-start.1
  23.4 9.2 %all_to_all.11.velocity_ref = f32[32,1,384]{2,1,0:T(1,128)S(1)} all-to-all(f32[32,1,384]{2,1,0:T(1,128)S(1)} %clump_update.1), channel_id=1, replica_groups=mesh['space'=16,'sub'=2] {'space','sub'}, dimensions={0} | all-to-all | bytes 98304 | tf_op jit(solution)/shard_map/all_to_all | solution.py:259
  32.5 0.0 copy-done
  32.5 0.0 copy-done.1
  32.5 0.9 %sphere_velocities.1 = (f32[6,128]{1,0:T(8,128)}, f32[3,4096]{1,0:T(4,128)}) custom-call(f32[32,1,384]{2,1,0:T(1,128)S(1)} %all_to_all.11.velocity_ref, f32[3,4096]{1,0:T(4,128)S(1)} %copy-done, s32[1,4096]{1,0:T(1,128)S(1)} %bitcast.3), custom_call_target="tpu_custom_call" | custom-call | tf_op jit(solution)/shard_map/sphere_velocities/pallas_call | solution.py:261
Async XLA Ops:
  7.7 15.6 %copy-start.2 = (f32[6,128]{1,0:T(8,128)S(1)}, f32[6,128]{1,0:T(8,128)}, u32[]{:S(2)}) copy-start(f32[6,128]{1,0:T(8,128)} %state_ref.1) | copy-start | bytes 9220
  7.7 15.6 %copy-start.3 = (f32[4,128]{1,0:T(4,128)S(1)}, f32[4,128]{1,0:T(4,128)}, u32[]{:S(2)}) copy-start(f32[4,128]{1,0:T(4,128)} %inverse_ref.1) | copy-start | bytes 6148
  23.3 9.2 %copy-start = (f32[3,4096]{1,0:T(4,128)S(1)}, f32[3,4096]{1,0:T(4,128)}, u32[]{:S(2)}) copy-start(f32[3,4096]{1,0:T(4,128)} %offset_ref.1) | copy-start | bytes 147460
  23.3 9.2 %copy-start.1 = (s32[4096]{0:T(1024)S(1)}, s32[4096]{0:T(1024)}, u32[]{:S(2)}) copy-start(s32[4096]{0:T(1024)} %param.13) | copy-start | bytes 49156
where the time goes:
time: 33.9 us; the launch traced here: 33.4 us
  blocking collectives  24.7 us (73%)
  Pallas kernels  7.36 us (22%)
  between operations  1.32 us (4%)
    all_to_all x1, blocking collectives, per_device(): lax.all_to_all(partial, axes, split_axis=0, concat_axis=0, tiled=True)  15.6 us
    all_to_all x1, blocking collectives, per_device(): lax.all_to_all(rows, axes, split_axis=0, concat_axis=0, tiled=True)  9.16 us
    pallas_call x1, Pallas kernels, per_device(): pl.pallas_call(loads_kernel, out_shape=pltpu.VMEM((devices, 1, 3 * clumps...  6.39 us
    pallas_call x1, Pallas kernels, per_device(): pl.pallas_call(velocity_kernel, out_shape=(jax.ShapeDtypeStruct((6, clump...  0.9 us

commit v1 on v0

--- a/solution.py
+++ b/solution.py
@@ -10,7 +10,7 @@
 
 TILE = 128
 SLOT = 256
-UNROLL = 8
+UNROLL = 4
 
 support_radius = 0.5
 press_coef = 4.0
@@ -53,7 +53,7 @@
 def loads_kernel(
     count_ref, list_hbm, fluid_hbm, sphere_hbm, offset_hbm, ids_hbm, out_ref,
     list_ref, fluid_ref, sphere_ref, offset_ref, ids_ref, arrived,
-    place_ref, wide_ref, terms_ref, weight_ref, acc_ref,
+    place_ref, lines_ref, lanes_ref, terms_ref, weight_ref, acc_ref,
 ):
     fluid_tiles = fluid_ref.shape[1] // TILE
     clumps = out_ref.shape[2] // 3
@@ -75,7 +75,7 @@
     acc_ref[...] = jnp.zeros_like(acc_ref)
     copies[0].wait()
 
-    @pl.loop(0, fluid_tiles, unroll=8)
+    @pl.loop(0, fluid_tiles, unroll=4)
     def _(tile):
         cols = pl.ds(pl.multiple_of(tile * TILE, TILE), TILE)
         state = fluid_ref[:, cols]
@@ -87,9 +87,14 @@
         high, low = split_two(jnp.concatenate([first, second], axis=0))
         both = jnp.concatenate([high, low], axis=0)
         terms_ref[tile] = jnp.concatenate([both, both], axis=1)
-        turned = state.T
-        for k in range(3):
-            wide_ref[k, cols, :] = jnp.broadcast_to(turned[:, k : k + 1], (TILE, TILE))
+
+    assert 3 * fluid_tiles <= TILE
+    lines_ref[...] = jnp.zeros_like(lines_ref)
+    for k in range(3):
+        for tile in range(fluid_tiles):
+            at = k * fluid_tiles + tile
+            lines_ref[at : at + 1, :] = fluid_ref[k : k + 1, tile * TILE : (tile + 1) * TILE]
+    lanes_ref[...] = lines_ref[...].T * (1.0 / support_radius) - 1.0
 
     copies[1].wait()
     place_ref[...] = sphere_ref[0:3, :] * (1.0 / support_radius) - 1.0
@@ -99,10 +104,14 @@
         a = list_ref[0, slot]
         b = list_ref[1, slot]
         cols = pl.ds(pl.multiple_of(a * TILE, TILE), TILE)
-        rows = pl.ds(pl.multiple_of(b * TILE, TILE), TILE)
-        dx = place_ref[0:1, cols] - wide_ref[0, rows, :]
-        dy = place_ref[1:2, cols] - wide_ref[1, rows, :]
-        dz = place_ref[2:3, cols] - wide_ref[2, rows, :]
+        lanes = lanes_ref[...]
+        dx, dy, dz = [
+            place_ref[k : k + 1, cols]
+            - jnp.take_along_axis(
+                lanes, jnp.full((TILE, TILE), k * fluid_tiles + b, jnp.int32), axis=1, mode="promise_in_bounds"
+            )
+            for k in range(3)
+        ]
         square = jnp.maximum(dx * dx + dy * dy + dz * dz, 1e-30)
         falloff = jnp.maximum(1.0 - square * lax.rsqrt(square), 0.0)
         high, low = split_two(falloff * falloff * falloff)
@@ -234,7 +243,8 @@
             pltpu.VMEM((1, spheres), jnp.int32),
             pltpu.SemaphoreType.DMA((5,)),
             pltpu.VMEM((3, spheres), f32),
-            pltpu.VMEM((3, fluid, TILE), f32),
+            pltpu.VMEM((TILE, TILE), f32),
+            pltpu.VMEM((TILE, TILE), f32),
             pltpu.VMEM((fluid // TILE, 32, 2 * TILE), bf16),
             pltpu.VMEM((UNROLL, 2 * TILE, TILE), bf16),
             pltpu.VMEM((16, spheres), f32),

time: 33.9 us -> 35.2 us (1.038)
  blocking collectives: 24.7 us -> 26.2 us
    all_to_all x1, blocking collectives: 15.6 us -> 17 us  [per_device(): lax.all_to_all(partial, axes, split_axis=0, concat_axis=0, tiled=True)]
where the time goes in v1:
time: 35.2 us; the launch traced here: 35 us
  blocking collectives  26.2 us (74%)
  Pallas kernels  7.5 us (21%)
  between operations  1.32 us (4%)
    all_to_all x1, blocking collectives, per_device(): lax.all_to_all(partial, axes, split_axis=0, concat_axis=0, tiled=True)  17 us
    all_to_all x1, blocking collectives, per_device(): lax.all_to_all(rows, axes, split_axis=0, concat_axis=0, tiled=True)  9.16 us
    pallas_call x1, Pallas kernels, per_device(): pl.pallas_call(loads_kernel, out_shape=pltpu.VMEM((devices, 1, 3 * clumps...  6.53 us
    pallas_call x1, Pallas kernels, per_device(): pl.pallas_call(velocity_kernel, out_shape=(jax.ShapeDtypeStruct((6, clump...  0.9 us

profile of v1, /device:TPU:0, one launch (start us, length us, event | category | flops | bytes accessed | tf_op | source)
XLA Modules:
  0.0 35.0 jit_solution(1599968263032894977)
XLA Ops:
  1.3 6.5 %clump_loads.1 = f32[32,1,384]{2,1,0:T(1,128)S(1)} custom-call(s32[1]{0:T(128)S(6)} %copy.10.count_ref, s32[2,128]{1,0:T(2,128)} %bitcast.4, f32[8,4096]{1,0:T(8,128)} %fluid_hbm.1, f32[7,4096]{1,0:T(8,128)} %sphere_hbm.1, f32[3,4096]{1,0:T(4,128)} %offset_ref.1, s32[1,4096]{1,0:T(1,128)} %bitcast.2), custom_call_target="tpu_custom_call" | custom-call | tf_op jit(solution)/shard_map/clump_loads/pallas_call | solution.py:233
  7.8 0.0 copy-start.2
  7.8 0.0 copy-start.3
  7.8 17.0 %all_to_all.10.arrived_ref = f32[32,1,384]{2,1,0:T(1,128)S(1)} all-to-all(f32[32,1,384]{2,1,0:T(1,128)S(1)} %clump_loads.1), channel_id=1, replica_groups=mesh['space'=16,'sub'=2] {'space','sub'}, dimensions={0} | all-to-all | bytes 98304 | tf_op jit(solution)/shard_map/all_to_all | solution.py:260
  24.8 0.0 copy-done.2
  24.8 0.0 copy-done.3
  24.9 0.1 clump_update.1
  24.9 0.0 copy-start
  24.9 0.0 copy-start.1
  24.9 9.2 %all_to_all.11.velocity_ref = f32[32,1,384]{2,1,0:T(1,128)S(1)} all-to-all(f32[32,1,384]{2,1,0:T(1,128)S(1)} %clump_update.1), channel_id=1, replica_groups=mesh['space'=16,'sub'=2] {'space','sub'}, dimensions={0} | all-to-all | bytes 98304 | tf_op jit(solution)/shard_map/all_to_all | solution.py:269
  34.1 0.0 copy-done
  34.1 0.0 copy-done.1
  34.1 0.9 %sphere_velocities.1 = (f32[6,128]{1,0:T(8,128)}, f32[3,4096]{1,0:T(4,128)}) custom-call(f32[32,1,384]{2,1,0:T(1,128)S(1)} %all_to_all.11.velocity_ref, f32[3,4096]{1,0:T(4,128)S(1)} %copy-done, s32[1,4096]{1,0:T(1,128)S(1)} %bitcast.3), custom_call_target="tpu_custom_call" | custom-call | tf_op jit(solution)/shard_map/sphere_velocities/pallas_call | solution.py:271
Async XLA Ops:
  7.8 17.0 %copy-start.2 = (f32[6,128]{1,0:T(8,128)S(1)}, f32[6,128]{1,0:T(8,128)}, u32[]{:S(2)}) copy-start(f32[6,128]{1,0:T(8,128)} %state_ref.1) | copy-start | bytes 9220
  7.8 17.0 %copy-start.3 = (f32[4,128]{1,0:T(4,128)S(1)}, f32[4,128]{1,0:T(4,128)}, u32[]{:S(2)}) copy-start(f32[4,128]{1,0:T(4,128)} %inverse_ref.1) | copy-start | bytes 6148
  24.9 9.2 %copy-start = (f32[3,4096]{1,0:T(4,128)S(1)}, f32[3,4096]{1,0:T(4,128)}, u32[]{:S(2)}) copy-start(f32[3,4096]{1,0:T(4,128)} %offset_ref.1) | copy-start | bytes 147460
  24.9 9.2 %copy-start.1 = (s32[4096]{0:T(1024)S(1)}, s32[4096]{0:T(1024)}, u32[]{:S(2)}) copy-start(s32[4096]{0:T(1024)} %param.13) | copy-start | bytes 49156

commit v2 on v0

--- a/solution.py
+++ b/solution.py
@@ -24,6 +24,12 @@
 def split_two(value):
     high = value.astype(bf16)
     return high, (value - high.astype(f32)).astype(bf16)
+
+
+def split_three(value):
+    high = value.astype(bf16).astype(f32)
+    middle = (value - high).astype(bf16).astype(f32)
+    return high, middle, (value - high) - middle
 
 
 def cross(left, right):
@@ -75,7 +81,12 @@
     acc_ref[...] = jnp.zeros_like(acc_ref)
     copies[0].wait()
 
-    @pl.loop(0, fluid_tiles, unroll=8)
+    row = lax.broadcasted_iota(jnp.int32, (TILE, TILE), 0)
+    column = lax.broadcasted_iota(jnp.int32, (TILE, TILE), 1)
+    unit = jnp.where(row == column, 1.0, 0.0).astype(bf16)
+    ones = jnp.ones((3 * TILE, TILE), bf16)
+
+    @pl.loop(0, fluid_tiles, unroll=4)
     def _(tile):
         cols = pl.ds(pl.multiple_of(tile * TILE, TILE), TILE)
         state = fluid_ref[:, cols]
@@ -87,9 +98,12 @@
         high, low = split_two(jnp.concatenate([first, second], axis=0))
         both = jnp.concatenate([high, low], axis=0)
         terms_ref[tile] = jnp.concatenate([both, both], axis=1)
-        turned = state.T
+        parts = [part.astype(bf16) for part in split_three(state[0:3])]
         for k in range(3):
-            wide_ref[k, cols, :] = jnp.broadcast_to(turned[:, k : k + 1], (TILE, TILE))
+            lines = [unit * jnp.broadcast_to(part[k : k + 1], (TILE, TILE)) for part in parts]
+            wide_ref[k, cols, :] = jnp.dot(
+                jnp.concatenate(lines, axis=1), ones, preferred_element_type=f32
+            )
 
     copies[1].wait()
     place_ref[...] = sphere_ref[0:3, :] * (1.0 / support_radius) - 1.0

time: 33.9 us -> 34.5 us (1.018)
  Pallas kernels: 7.36 us -> 9.31 us
  blocking collectives: 24.7 us -> 23.6 us
    pallas_call x1, Pallas kernels: 6.39 us -> 8.34 us  [per_device(): pl.pallas_call(loads_kernel, out_shape=pltpu.VMEM((devices, 1, 3 * clumps...]
    all_to_all x1, blocking collectives: 15.6 us -> 14.4 us  [per_device(): lax.all_to_all(partial, axes, split_axis=0, concat_axis=0, tiled=True)]
where the time goes in v2:
time: 34.5 us; the launch traced here: 34.3 us
  blocking collectives  23.6 us (68%)
  Pallas kernels  9.31 us (27%)
  between operations  1.32 us (4%)
    all_to_all x1, blocking collectives, per_device(): lax.all_to_all(partial, axes, split_axis=0, concat_axis=0, tiled=True)  14.4 us
    all_to_all x1, blocking collectives, per_device(): lax.all_to_all(rows, axes, split_axis=0, concat_axis=0, tiled=True)  9.16 us
    pallas_call x1, Pallas kernels, per_device(): pl.pallas_call(loads_kernel, out_shape=pltpu.VMEM((devices, 1, 3 * clumps...  8.34 us
    pallas_call x1, Pallas kernels, per_device(): pl.pallas_call(velocity_kernel, out_shape=(jax.ShapeDtypeStruct((6, clump...  0.9 us

profile of v2, /device:TPU:0, one launch (start us, length us, event | category | flops | bytes accessed | tf_op | source)
XLA Modules:
  0.0 34.3 jit_solution(5664665618061342767)
XLA Ops:
  1.3 8.3 %clump_loads.1 = f32[32,1,384]{2,1,0:T(1,128)S(1)} custom-call(s32[1]{0:T(128)S(6)} %copy.10.count_ref, s32[2,128]{1,0:T(2,128)} %bitcast.4, f32[8,4096]{1,0:T(8,128)} %fluid_hbm.1, f32[7,4096]{1,0:T(8,128)} %sphere_hbm.1, f32[3,4096]{1,0:T(4,128)} %offset_ref.1, s32[1,4096]{1,0:T(1,128)} %bitcast.2), custom_call_target="tpu_custom_call" | custom-call | tf_op jit(solution)/shard_map/clump_loads/pallas_call | solution.py:238
  9.6 0.0 copy-start.2
  9.6 0.0 copy-start.3
  9.7 14.4 %all_to_all.10.arrived_ref = f32[32,1,384]{2,1,0:T(1,128)S(1)} all-to-all(f32[32,1,384]{2,1,0:T(1,128)S(1)} %clump_loads.1), channel_id=1, replica_groups=mesh['space'=16,'sub'=2] {'space','sub'}, dimensions={0} | all-to-all | bytes 98304 | tf_op jit(solution)/shard_map/all_to_all | solution.py:264
  24.1 0.0 copy-done.2
  24.1 0.0 copy-done.3
  24.1 0.1 clump_update.1
  24.2 0.0 copy-start
  24.2 0.0 copy-start.1
  24.2 9.2 %all_to_all.11.velocity_ref = f32[32,1,384]{2,1,0:T(1,128)S(1)} all-to-all(f32[32,1,384]{2,1,0:T(1,128)S(1)} %clump_update.1), channel_id=1, replica_groups=mesh['space'=16,'sub'=2] {'space','sub'}, dimensions={0} | all-to-all | bytes 98304 | tf_op jit(solution)/shard_map/all_to_all | solution.py:273
  33.3 0.0 copy-done
  33.3 0.0 copy-done.1
  33.4 0.9 %sphere_velocities.1 = (f32[6,128]{1,0:T(8,128)}, f32[3,4096]{1,0:T(4,128)}) custom-call(f32[32,1,384]{2,1,0:T(1,128)S(1)} %all_to_all.11.velocity_ref, f32[3,4096]{1,0:T(4,128)S(1)} %copy-done, s32[1,4096]{1,0:T(1,128)S(1)} %bitcast.3), custom_call_target="tpu_custom_call" | custom-call | tf_op jit(solution)/shard_map/sphere_velocities/pallas_call | solution.py:275
Async XLA Ops:
  9.6 14.5 %copy-start.2 = (f32[6,128]{1,0:T(8,128)S(1)}, f32[6,128]{1,0:T(8,128)}, u32[]{:S(2)}) copy-start(f32[6,128]{1,0:T(8,128)} %state_ref.1) | copy-start | bytes 9220
  9.6 14.5 %copy-start.3 = (f32[4,128]{1,0:T(4,128)S(1)}, f32[4,128]{1,0:T(4,128)}, u32[]{:S(2)}) copy-start(f32[4,128]{1,0:T(4,128)} %inverse_ref.1) | copy-start | bytes 6148
  24.2 9.2 %copy-start = (f32[3,4096]{1,0:T(4,128)S(1)}, f32[3,4096]{1,0:T(4,128)}, u32[]{:S(2)}) copy-start(f32[3,4096]{1,0:T(4,128)} %offset_ref.1) | copy-start | bytes 147460
  24.2 9.2 %copy-start.1 = (s32[4096]{0:T(1024)S(1)}, s32[4096]{0:T(1024)}, u32[]{:S(2)}) copy-start(s32[4096]{0:T(1024)} %param.13) | copy-start | bytes 49156
